TPU v7x, 512 devices: a whole 4x4x16 slice. The times are simulated.
512 devices in a mesh: row: 16 (over z), col: 32 (over y, x, core).
Axes of the slice: x: 4, y: 4, z: 16, core: 2. Of those that a mesh axis runs over, the one named last changes fastest.
Arguments:
- inputs: bfloat16 [768, 12288], P('col', 'row'), may hold values from -40 to 40
- ln_gain: float32 [12288], P('row'), may hold values from 0.25 to 1.75
- ln_bias: float32 [12288], P('row'), may hold values from -4 to 4
- w_up: bfloat16 [12288, 49152], P('row', 'col'), may hold values from -0.0546875 to 0.0546875
- up_bias: float32 [49152], P('col'), may hold values from -4 to 4
- w_down: bfloat16 [49152, 12288], P('col', 'row'), may hold values from -0.02734375 to 0.02734375
- down_bias: float32 [12288], P('row'), may hold values from -4 to 4
Outputs:
- block_out: bfloat16 [768, 12288], P('col', 'row')
All inputs are finite; a program needn't handle non-finite values.
Results may differ from a plain program's by a relative error of at most 0.0085.
Values may be sent and summed in bfloat16 or wider, within the bound.
A program may use at most 64 MiB of HBM per device.

v0:
```python
import jax
import jax.numpy as jnp
from jax import lax
from jax.sharding import PartitionSpec as P

D = 12288


def local(inputs, ln_gain, ln_bias, w_up, up_bias, w_down, down_bias):
    in_float = inputs.astype(jnp.float32)
    total = lax.psum(jnp.sum(in_float, axis=1), "row")
    average = total / D
    centered = in_float - average[:, None]
    spread = lax.psum(jnp.sum(centered * centered, axis=1), "row")
    variance = spread / D
    normed = (centered * lax.rsqrt(variance + 1e-05)[:, None] * ln_gain + ln_bias).astype(
        jnp.bfloat16
    )
    gathered = lax.all_gather(normed, "col", axis=0, tiled=True)
    summed = lax.psum_scatter(
        jnp.dot(gathered, w_up, preferred_element_type=jnp.float32).astype(jnp.bfloat16),
        "row",
        scatter_dimension=0,
        tiled=True,
    ).astype(jnp.float32)
    hidden = jax.nn.gelu(summed + up_bias, approximate=True).astype(jnp.bfloat16)
    terms = jnp.dot(
        lax.all_gather(hidden, "row", axis=0, tiled=True),
        w_down,
        preferred_element_type=jnp.float32,
    )
    down_sum = lax.psum_scatter(
        terms.astype(jnp.bfloat16), "col", scatter_dimension=0, tiled=True
    ).astype(jnp.float32)
    return (in_float + down_sum + down_bias).astype(jnp.bfloat16)


def solution(mesh):
    placed = (
        P("col", "row"),
        P("row"),
        P("row"),
        P("row", "col"),
        P("col"),
        P("col", "row"),
        P("row"),
    )
    return jax.shard_map(
        local, mesh=mesh, in_specs=placed, out_specs=P("col", "row"), check_vma=False
    )
```

profile of v0, /device:TPU:7, one launch (start us, length us, event | category | flops | bytes accessed | tf_op | source)
XLA Modules:
  0.0 387.9 jit_solution(8472920669554600024)
XLA Ops:
  6.5 0.0 copy-start
  6.5 0.0 all-gather.3.cloned.1.call-start
  6.5 1.0 convert_reduce_fusion
  7.6 29.5 %psum.14 = f32[24]{0:T(128)S(1)} all-reduce(f32[24]{0:T(128)S(1)} %convert_reduce_fusion), channel_id=1, replica_groups=mesh['row'=16,'col'=32] {'row'}, use_global_device_ids=true, to_apply=%region_1.0 | all-reduce | flops 24 | bytes 192 | tf_op jit(solution)/shard_map/psum | solution.py:11
  37.1 1.0 fusion.10
  38.0 20.6 %psum.15 = f32[24]{0:T(128)S(1)} all-reduce(f32[24]{0:T(128)S(1)} %fusion.10), channel_id=1, replica_groups=mesh['row'=16,'col'=32] {'row'}, use_global_device_ids=true, to_apply=%region_3.0 | all-reduce | flops 24 | bytes 192 | tf_op jit(solution)/shard_map/psum | solution.py:14
  58.6 1.5 fusion.13
  60.1 0.0 all-gather.3.cloned.1.call-update
  60.2 0.0 reduce-scatter.3.cloned.1.call-start
  60.2 68.8 %all-gather.3.cloned.1.call-done = bf16[768,768]{1,0:T(8,128)(2,1)} async-done(((bf16[24,768]{1,0:T(8,128)(2,1)}), bf16[768,768]{1,0:T(8,128)(2,1)}) %all-gather.3.cloned.1.call-update) | async-done | bytes 1179664 | tf_op jit(solution)/shard_map/all_gather | solution.py:19
  129.0 4.7 %convolution_convert_fusion = bf16[768,1536]{1,0:T(8,128)(2,1)} fusion(bf16[768,768]{1,0:T(8,128)(2,1)} %all-gather.3.cloned.1.call-done, bf16[768,1536]{1,0:T(8,128)(2,1)S(1)} %copy-done), kind=kOutput, calls=%fused_computation | convolution fusion | flops 1813118976 | bytes 5898240 | tf_op jit(solution)/shard_map/dot_general | solution.py:21
  133.7 0.0 reduce-scatter.3.cloned.1.call-update
  133.8 0.0 all-gather.5.cloned.1.call-start
  133.8 63.3 %reduce-scatter.3.cloned.1.call-done = bf16[48,1536]{1,0:T(8,128)(2,1)} async-done(((bf16[768,1536]{1,0:T(8,128)(2,1)}), bf16[48,1536]{1,0:T(8,128)(2,1)}) %reduce-scatter.3.cloned.1.call-update) | async-done | bytes 147472 | tf_op jit(solution)/shard_map/reduce_scatter | solution.py:20
  197.1 1.7 fusion.7
  198.8 0.0 all-gather.5.cloned.1.call-update
  198.8 0.0 copy-start.1
  198.8 0.0 copy-start.3
  198.8 0.0 reduce-scatter.5.cloned.1.call-start
  198.9 73.2 %all-gather.5.cloned.1.call-done = bf16[768,1536]{1,0:T(8,128)(2,1)} async-done(((bf16[48,1536]{1,0:T(8,128)(2,1)}), bf16[768,1536]{1,0:T(8,128)(2,1)}) %all-gather.5.cloned.1.call-update) | async-done | bytes 2359312 | tf_op jit(solution)/shard_map/all_gather | solution.py:28
  272.1 5.4 %convolution_convert_fusion.1 = bf16[768,768]{1,0:T(8,128)(2,1)} fusion(bf16[768,1536]{1,0:T(8,128)(2,1)} %all-gather.5.cloned.1.call-done, bf16[1536,768]{1,0:T(8,128)(2,1)} %param.12), kind=kOutput, calls=%fused_computation.1 | convolution fusion | flops 1812529152 | bytes 5898240 | tf_op jit(solution)/shard_map/dot_general | solution.py:27
  277.5 0.0 reduce-scatter.5.cloned.1.call-update
  277.5 102.5 %reduce-scatter.5.cloned.1.call-done = bf16[24,768]{1,0:T(8,128)(2,1)} async-done(((bf16[768,768]{1,0:T(8,128)(2,1)}), bf16[24,768]{1,0:T(8,128)(2,1)}) %reduce-scatter.5.cloned.1.call-update) | async-done | bytes 36880 | tf_op jit(solution)/shard_map/reduce_scatter | solution.py:32
  380.0 1.4 fusion.15
  (7 shorter events, 0.0 us)
Async XLA Ops:
  6.5 122.5 %copy-start = (bf16[768,1536]{1,0:T(8,128)(2,1)S(1)}, bf16[768,1536]{1,0:T(8,128)(2,1)}, u32[]{:S(2)}) copy-start(bf16[768,1536]{1,0:T(8,128)(2,1)} %param.10) | copy-start | bytes 7077892
  6.5 122.5 %all-gather.3.cloned.1.call-start = ((), (), s32[]{:S(2)}) async-start(), calls=%async_computation.2 | async-start | bytes 1216512 | tf_op jit(solution)/shard_map/all_gather | solution.py:19
  60.2 136.9 %reduce-scatter.3.cloned.1.call-start = ((), (), s32[]{:S(2)}) async-start(), calls=%async_computation.3 | async-start | bytes 2506752 | tf_op jit(solution)/shard_map/reduce_scatter | solution.py:20
  133.7 63.4 %copy-start.2 = (f32[1536]{0:T(1024)S(1)}, f32[1536]{0:T(1024)}, u32[]{:S(2)}) copy-start(f32[1536]{0:T(1024)} %param.11) | copy-start | bytes 18436
  133.8 138.3 %all-gather.5.cloned.1.call-start = ((), (), s32[]{:S(2)}) async-start(), calls=%async_computation.4 | async-start | bytes 2506752 | tf_op jit(solution)/shard_map/all_gather | solution.py:28
  198.8 181.2 %copy-start.1 = (bf16[24,768]{1,0:T(8,128)(2,1)S(1)}, bf16[24,768]{1,0:T(8,128)(2,1)}, u32[]{:S(2)}) copy-start(bf16[24,768]{1,0:T(8,128)(2,1)} %param.7) | copy-start | bytes 110596
  198.8 181.2 %copy-start.3 = (f32[768]{0:T(1024)S(1)}, f32[768]{0:T(1024)}, u32[]{:S(2)}) copy-start(f32[768]{0:T(1024)} %param.13) | copy-start | bytes 9220
  198.8 181.2 %reduce-scatter.5.cloned.1.call-start = ((), (), s32[]{:S(2)}) async-start(), calls=%async_computation.5 | async-start | bytes 1216512 | tf_op jit(solution)/shard_map/reduce_scatter | solution.py:32
Sparse Core Ops, SparseCore 0:
  60.3 68.7 all-gather.2
  133.9 63.1 reduce-scatter.2
  199.2 72.8 all-gather.4
  277.6 102.3 reduce-scatter.4
where the time goes:
time: 391 us; the launch traced here: 388 us
  waiting for transfers between devices  308 us (79%)
  blocking collectives  50.1 us (13%)
  between operations  13.1 us (3%)
  matrix products  10.1 us (3%)
  other arithmetic  6.57 us (2%)
    reduce_scatter x1, waiting for transfers between devices, local(): lax.psum_scatter(terms.astype(jnp.bfloat16), 'col', scatter_dimension=0,...  103 us
    all_gather x1, waiting for transfers between devices, local(): lax.all_gather(hidden, 'row', axis=0, tiled=True)  73.2 us
    all_gather x1, waiting for transfers between devices, local(): gathered = lax.all_gather(normed, 'col', axis=0, tiled=True)  68.8 us
    reduce_scatter x1, waiting for transfers between devices, local(): lax.psum_scatter(jnp.dot(gathered, w_up, preferred_element_type=jnp.float...  63.3 us
    psum x1, blocking collectives, local(): total = lax.psum(jnp.sum(in_float, axis=1), 'row')  29.5 us
    psum x1, blocking collectives, local(): spread = lax.psum(jnp.sum(centered * centered, axis=1), 'row')  20.6 us
  transfers between devices with their start and end apart: 4, of which 4 were waited for; matrix products, arithmetic and copies ran while one was open for 0% of the time, Pallas kernels for 0%

commit v1 on v0

v1 whole, which is shorter than its diff:
```python
import functools

import jax
import jax.numpy as jnp
from jax import lax
from jax.experimental import pallas as pl
from jax.experimental.pallas import tpu as pltpu
from jax.sharding import PartitionSpec as P

F32, BF16 = jnp.float32, jnp.bfloat16
MESH = pl.DeviceIdType.MESH
EPS = 1e-05
J = 4
SPLIT = ((0, 1), (2, 3))
RS_ORDER = ((2, 3, 0, 1), (0, 1, 2, 3))
AG_ORDER = ((0, 1, 2, 3), (2, 3, 0, 1))
GROUPS = 3


def kernel(
    n,
    x_ref, gain_ref, bias_ref, ub_ref, db_ref, wu_hbm, wd_hbm,
    out_ref,
    wu, wd, xg, pbuf, lm, lm2, st_out, st_in, gb, gb_in, rs_out, rs_in, ag_own, ag_in,
    tb, pair_out, pair_in, star_out, star_in,
    w_sem, x_ss, x_rs, st_ss, st_rs, gb_ss, gb_rs, r_ss, r_rs, a_ss, a_rs, p_ss, p_rs, s_ss, s_rs,
):
    half = n // 2
    feat, unit = wu.shape
    width = unit // J
    rows = 2 * GROUPS * 8
    z, c = lax.axis_index("row"), lax.axis_index("col")
    q, e = c // 2, lax.rem(c, 2)
    offs = tuple(p * (n // GROUPS) for p in range(GROUPS))
    sibling = (z, c + 1 - 2 * e)
    along = ((lax.rem(z + 1, n), c), (lax.rem(z + n - 1, n), c))
    lane = lax.broadcasted_iota(jnp.int32, (8, 128), 1)
    head = lane < 2 * GROUPS

    def remote(src, dst, ss, rs, to):
        return pltpu.make_async_remote_copy(
            src_ref=src, dst_ref=dst, send_sem=ss, recv_sem=rs, device_id=to, device_id_type=MESH
        )

    def drain(ref, sem):
        pltpu.make_async_copy(ref, ref, sem).wait()

    load_up = pltpu.make_async_copy(wu_hbm, wu, w_sem.at[0])
    load_down = pltpu.make_async_copy(wd_hbm, wd, w_sem.at[1])
    load_up.start()
    load_down.start()

    barrier = pltpu.get_barrier_semaphore()
    for to in along:
        pl.semaphore_signal(barrier, inc=1, device_id=to, device_id_type=MESH)

    def greet(i, carry):
        to = (z, lax.rem(c + i, 2 * n))
        pl.semaphore_signal(barrier, inc=1, device_id=to, device_id_type=MESH)
        return carry

    lax.fori_loop(1, 2 * n, greet, 0)
    pl.semaphore_wait(barrier, 2 * n + 1)

    def spread(far):
        for p in range(GROUPS):
            k = lax.rem(q + offs[p], n)
            dist = jnp.minimum(lax.rem(k - z + n, n), lax.rem(z - k + n, n))

            @pl.when(dist == far)
            def _():
                place = xg.at[k * 2 * GROUPS + e * GROUPS + p]
                pltpu.make_async_copy(x_ref.at[p], place, x_rs.at[k]).start()

                def send(i, carry):
                    to = (z, lax.rem(c + i, 2 * n))
                    remote(x_ref.at[p], place, x_ss, x_rs.at[k], to).start()
                    return carry

                lax.fori_loop(1, 2 * n, send, 0)

    def columns(tile):
        return jnp.concatenate([tile[:, g : g + 1][None] for g in range(2 * GROUPS)], axis=0)

    def centered(k, d):
        at = pl.ds(k * 2 * GROUPS, 2 * GROUPS)
        x = xg[at].astype(F32)
        mean = jnp.sum(x, axis=2, keepdims=True) * (1.0 / feat)
        x = x - mean
        square = jnp.sum(x * x, axis=2, keepdims=True)
        m_tile = jnp.zeros((8, 128), F32)
        s_tile = jnp.zeros((8, 128), F32)
        for g in range(2 * GROUPS):
            m_tile = jnp.where(lane == g, mean[g], m_tile)
            s_tile = jnp.where(lane == g, square[g], s_tile)
        lm[d] = m_tile
        lm2[d] = s_tile
        return (x * gain_ref[...][None]).reshape(rows, feat).astype(BF16)

    def chunk(d, s):
        return lax.rem(z + n + half - s, n) if d == 0 else lax.rem(z + half + s, n)

    def wait_inputs(k):
        drain(xg.at[pl.ds(k * 2 * GROUPS, 2 * GROUPS)], x_rs.at[k])

    def products(s):
        wait_inputs(chunk(0, s))

        @pl.when(s < half)
        def _():
            wait_inputs(chunk(1, s))

        both = jnp.concatenate([centered(chunk(0, s), 0), centered(chunk(1, s), 1)], axis=0)
        for i in range(3):
            cols = slice(i * (unit // 3), (i + 1) * (unit // 3))
            pbuf[:, cols] = jnp.dot(both, wu[:, cols], preferred_element_type=F32)

    def st_copy(d, s):
        return remote(st_out.at[d, s], st_in.at[d, s], st_ss, st_rs.at[d, s], along[d])

    def rs_copy(d, s, j):
        at = (d * half + s) * J + j
        return remote(rs_out.at[at], rs_in.at[at], r_ss, r_rs.at[d, s, j], along[d])

    def gb_copy(d, s, src):
        return remote(src, gb_in.at[d * half + s], gb_ss, gb_rs.at[d, s], along[d])

    def row_of(ref_value, first, j):
        per = width // 128
        return jnp.concatenate(
            [ref_value[first + j * per + i : first + j * per + i + 1] for i in range(per)], axis=1
        )

    per_row = unit // 128
    zero = jnp.zeros((rows, width), BF16)
    for d in range(2):
        for j in SPLIT[1 - d]:
            rs_in[d * half * J + j] = zero

    spread(half)
    spread(half - 1)
    spread(half - 2)

    load_up.wait()
    sub = lax.broadcasted_iota(jnp.int32, (16, feat), 0)
    gain, bias = gain_ref[...], bias_ref[...]
    gain_hi, bias_hi = gain.astype(BF16).astype(F32), bias.astype(BF16).astype(F32)
    lhs = jnp.where(
        sub == 0,
        gain_hi,
        jnp.where(
            sub == 1,
            gain - gain_hi,
            jnp.where(sub == 2, bias_hi, jnp.where(sub == 3, bias - bias_hi, 0.0)),
        ),
    ).astype(BF16)
    sums = jnp.dot(lhs, wu[...], preferred_element_type=F32)
    for i in range(per_row):
        cols = slice(i * 128, (i + 1) * 128)
        gb[i : i + 1] = sums[0:1, cols] + sums[1:2, cols]
        gb[per_row + i : per_row + i + 1] = sums[2:3, cols] + sums[3:4, cols]

    first = chunk(0, 0)
    wait_inputs(first)
    start = centered(first, 0)
    st_out[0, 0] = lm[0] + pltpu.roll(lm2[0], 64, 1)
    st_out[1, 0] = lm[0]
    for d in range(2):
        st_copy(d, 0).start()
    for i in range(2):
        for d in range(2):
            j = SPLIT[d][i]
            part = jnp.dot(start, wu[:, j * width : (j + 1) * width], preferred_element_type=F32)
            rs_out[d * half * J + j] = part.astype(BF16)
            rs_copy(d, 0, j).start()
    for d in range(2):
        gb_copy(d, 0, gb).start()
    products(1)

    def rs_step(s, carry):
        shift = []
        for d in range(2):
            st_copy(d, s - 1).wait_recv()
            got = st_in[d, s - 1]
            off = jnp.where(head, lm[d] - got, 0.0)
            square = jnp.where(head, lm2[d] + feat * off * off, 0.0)
            st_out[d, s] = got + pltpu.roll(off, 32, 1) + pltpu.roll(square, 64, 1)
            st_copy(d, s).start()
            shift.append(columns(off))
        own = gb[...]
        for i in range(J):
            for d in range(2):
                j = RS_ORDER[d][i]
                if i < 2:
                    pl.when(s > 1)(lambda d=d, j=j: rs_copy(d, s - 1, j).wait_recv())
                else:
                    rs_copy(d, s - 1, j).wait_recv()
                got = rs_in[(d * half + s - 1) * J + j].astype(F32).reshape(2 * GROUPS, 8, width)
                mine = pbuf[d * rows : (d + 1) * rows, j * width : (j + 1) * width]
                total = got + mine.reshape(2 * GROUPS, 8, width) + shift[d] * row_of(own, 0, j)[None]
                rs_out[(d * half + s) * J + j] = total.reshape(rows, width).astype(BF16)
                rs_copy(d, s, j).start()
        gb_copy(0, s - 1, gb).wait_recv()
        gb_copy(0, s, gb_in.at[s - 1]).start()
        gb_copy(1, s - 1, gb).wait_recv()

        @pl.when(s < half - 1)
        def _():
            gb_copy(1, s, gb_in.at[half + s - 1]).start()

        spread(half - 2 - s)
        products(s + 1)
        return carry

    lax.fori_loop(1, half, rs_step, 0)

    def ag_copy(d, s, j, src):
        at = (d * half + s) * J + j
        return remote(src, ag_in.at[at], a_ss, a_rs.at[d, s, j], along[d])

    gb_copy(0, half - 1, gb).wait_recv()
    load_down.wait()
    gb_all = gb[...]
    for i in range(2 * half - 1):
        gb_all = gb_all + gb_in[i]
    own = gb[...]
    for d in range(2):
        st_copy(d, half - 1).wait_recv()
    up, down = st_in[0, half - 1], st_in[1, half - 1]
    off = jnp.where(head, lm[0] - up, 0.0)
    mean_off = (pltpu.roll(up + down, 96, 1) + off) * (1.0 / n)
    square = pltpu.roll(up + down, 64, 1) + lm2[0] + feat * off * off
    scale = lax.rsqrt(square * (1.0 / (n * feat)) - mean_off * mean_off + EPS)
    off_c, mean_c, scale_c = columns(off), columns(mean_off), columns(scale)
    for j in range(J):
        cols = slice(j * width, (j + 1) * width)
        total = pbuf[0:rows, cols].reshape(2 * GROUPS, 8, width)
        for d in range(2):
            rs_copy(d, half - 1, j).wait_recv()
            got = rs_in[(d * half + half - 1) * J + j]
            total = total + got.astype(F32).reshape(2 * GROUPS, 8, width)
        total = total + off_c * row_of(own, 0, j)[None] - mean_c * row_of(gb_all, 0, j)[None]
        v = total * scale_c + row_of(gb_all, per_row, j)[None] + ub_ref[:, cols][None]
        hidden = jax.nn.gelu(v, approximate=True)
        ag_own[j] = hidden.reshape(rows, width).astype(BF16)
        for d in range(2):
            ag_copy(d, 0, j, ag_own.at[j]).start()

    def pair_copy(k):
        return remote(pair_out.at[k], pair_in.at[k], p_ss, p_rs.at[k], sibling)

    def to_pair(k, value):
        tb[k] = value.reshape(2 * GROUPS, 8, feat)
        pair_out[k] = tb[k, pl.ds((1 - e) * GROUPS, GROUPS)].astype(BF16)
        pair_copy(k).start()

    def to_owner(k):
        pair_copy(k).wait_recv()
        star_out[k] = (tb[k, pl.ds(e * GROUPS, GROUPS)] + pair_in[k].astype(F32)).astype(BF16)
        for p in range(GROUPS):
            owner = lax.rem(k - offs[p] + n, n)
            place = star_in.at[p * n + q]

            @pl.when(owner == q)
            def _():
                pltpu.make_async_copy(star_out.at[k, p], place, s_rs).start()

            @pl.when(owner != q)
            def _():
                remote(star_out.at[k, p], place, s_ss, s_rs, (z, 2 * owner + e)).start()

    def down_product(pieces):
        return jnp.dot(jnp.concatenate(pieces, axis=1), wd[...], preferred_element_type=F32)

    to_pair(z, down_product([ag_own[j] for j in range(J)]))

    def ag_step(s, carry):
        for i in range(J):
            for d in range(2):
                j = AG_ORDER[d][i]
                ag_copy(d, s, j, ag_own.at[j]).wait_recv()
                held = ag_in.at[(d * half + s) * J + j]
                if i < 2:
                    ag_copy(d, s + 1, j, held).start()
                else:
                    pl.when(s < half - 2)(lambda d=d, j=j, held=held: ag_copy(d, s + 1, j, held).start())
        to_owner(lax.rem(z - s + n, n))
        pl.when(s > 0)(lambda: to_owner(lax.rem(z + s, n)))
        value = down_product(
            [
                jnp.concatenate([ag_in[s * J + j], ag_in[(half + s) * J + j]], axis=0)
                for j in range(J)
            ]
        )
        to_pair(lax.rem(z - 1 - s + n, n), value[:rows])
        to_pair(lax.rem(z + 1 + s, n), value[rows:])
        return carry

    lax.fori_loop(0, half - 1, ag_step, 0)
    to_owner(lax.rem(z + 1 + half, n))
    to_owner(lax.rem(z + half - 1, n))
    pieces = []
    for d in range(2):
        for j in SPLIT[d]:
            ag_copy(d, half - 1, j, ag_own.at[j]).wait_recv()
            pieces.append(ag_in[(d * half + half - 1) * J + j])
    last = lax.rem(z + half, n)
    to_pair(last, down_product(pieces))
    to_owner(last)

    drain(star_in, s_rs)
    for p in range(GROUPS):
        total = jnp.sum(star_in[p * n : (p + 1) * n].astype(F32), axis=0)
        out_ref[p] = (x_ref[p].astype(F32) + total + db_ref[...]).astype(BF16)

    drain(xg.at[pl.ds(0, GROUPS * (2 * n - 1))], x_ss)
    drain(st_in, st_ss)
    drain(gb_in.at[pl.ds(0, n - 1)], gb_ss)
    drain(rs_in.at[pl.ds(0, (n - 1) * J)], r_ss)
    drain(ag_in.at[pl.ds(0, (n - 1) * J)], a_ss)
    drain(pair_in, p_ss)
    drain(star_in.at[pl.ds(0, GROUPS * (n - 1))], s_ss)


def local(n, inputs, ln_gain, ln_bias, w_up, up_bias, w_down, down_bias):
    feat, unit = w_up.shape
    half, rows, width = n // 2, 2 * GROUPS * 8, unit // J
    vmem, hbm = pl.BlockSpec(memory_space=pltpu.VMEM), pl.BlockSpec(memory_space=pl.ANY)
    sem = pltpu.SemaphoreType.DMA
    out = pl.pallas_call(
        functools.partial(kernel, n),
        out_shape=jax.ShapeDtypeStruct((GROUPS, 8, feat), BF16),
        in_specs=[vmem] * 5 + [hbm] * 2,
        out_specs=vmem,
        scratch_shapes=[
            pltpu.VMEM((feat, unit), BF16),
            pltpu.VMEM((unit, feat), BF16),
            pltpu.VMEM((n * 2 * GROUPS, 8, feat), BF16),
            pltpu.VMEM((2 * rows, unit), F32),
            pltpu.VMEM((2, 8, 128), F32),
            pltpu.VMEM((2, 8, 128), F32),
            pltpu.VMEM((2, half, 8, 128), F32),
            pltpu.VMEM((2, half, 8, 128), F32),
            pltpu.VMEM((2 * unit // 128, 128), F32),
            pltpu.VMEM((n, 2 * unit // 128, 128), F32),
            pltpu.VMEM((2 * half * J, rows, width), BF16),
            pltpu.VMEM((2 * half * J, rows, width), BF16),
            pltpu.VMEM((J, rows, width), BF16),
            pltpu.VMEM((2 * half * J, rows, width), BF16),
            pltpu.VMEM((n, 2 * GROUPS, 8, feat), F32),
            pltpu.VMEM((n, GROUPS, 8, feat), BF16),
            pltpu.VMEM((n, GROUPS, 8, feat), BF16),
            pltpu.VMEM((n, GROUPS, 8, feat), BF16),
            pltpu.VMEM((GROUPS * n, 8, feat), BF16),
            sem((2,)),
            sem,
            sem((n,)),
            sem,
            sem((2, half)),
            sem,
            sem((2, half)),
            sem,
            sem((2, half, J)),
            sem,
            sem((2, half, J)),
            sem,
            sem((n,)),
            sem,
            sem,
        ],
        compiler_params=pltpu.CompilerParams(
            collective_id=0, has_side_effects=True, vmem_limit_bytes=50 << 20
        ),
    )(
        inputs.reshape(GROUPS, 8, feat),
        ln_gain[None],
        ln_bias[None],
        up_bias[None],
        down_bias[None],
        w_up,
        w_down,
    )
    return out.reshape(GROUPS * 8, feat)


def solution(mesh):
    placed = (
        P("col", "row"),
        P("row"),
        P("row"),
        P("row", "col"),
        P("col"),
        P("col", "row"),
        P("row"),
    )
    return jax.shard_map(
        functools.partial(local, mesh.shape["row"]),
        mesh=mesh,
        in_specs=placed,
        out_specs=P("col", "row"),
        check_vma=False,
    )
```

time: 391 us -> 104 us (0.27)
  waiting for transfers between devices: 308 us -> 0 us
  Pallas kernels: 0 us -> 97.4 us
  blocking collectives: 50.1 us -> 0 us
  between operations: 13.1 us -> 0.01 us
  matrix products: 10.1 us -> 0 us
  other arithmetic: 6.57 us -> 0 us
  local copies, waits for them, and re-layouts: 0.02 us -> 5.82 us
    reduce_scatter x2 -> x0, waiting for transfers between devices: 166 us -> none  [the longest x1 103 us: local(): lax.psum_scatter(terms.astype(jnp.bfloat16), 'col', scatter_dimension=0,...]
    all_gather x2 -> x0, waiting for transfers between devices: 142 us -> none  [the longest x1 73.2 us: local(): lax.all_gather(hidden, 'row', axis=0, tiled=True)]
    pallas_call x0 -> x1, Pallas kernels: none -> 97.4 us  [local(): pl.pallas_call(functools.partial(kernel, n), out_shape=jax.ShapeDtypeStru...]
    psum x2 -> x0, blocking collectives: 50.1 us -> none  [the longest x1 29.5 us: local(): total = lax.psum(jnp.sum(in_float, axis=1), 'row')]
    dot_general x2 -> x0, matrix products: 10.1 us -> none  [the longest x1 5.38 us: local(): jnp.dot(lax.all_gather(hidden, 'row', axis=0, tiled=True), w_down, prefer...]
    convert_element_type x3 -> x0, other arithmetic: 4.58 us -> none  [the longest x1 1.69 us: local(): jax.nn.gelu(summed + up_bias, approximate=True).astype(jnp.bfloat16)]
  transfers between devices with their start and end apart: 4 -> 0, of which waited for: 4 -> 0; matrix products, arithmetic and copies ran while one was open for 0% -> 0% of each run, Pallas kernels for 0% -> 0%
where the time goes in v1:
time: 104 us; the launch traced here: 103 us
  Pallas kernels  97.4 us (94%)
  local copies, waits for them, and re-layouts  5.82 us (6%)
    pallas_call x1, Pallas kernels, local(): pl.pallas_call(functools.partial(kernel, n), out_shape=jax.ShapeDtypeStru...  97.4 us
    unnamed x5, local copies, waits for them, and re-layouts  3.05 us

profile of v1, /device:TPU:7, one launch (start us, length us, event | category | flops | bytes accessed | tf_op | source)
XLA Modules:
  0.0 103.3 jit_solution(6049690992624146374)
XLA Ops:
  0.0 0.7 broadcast_in_dim.12.gain_ref
  0.7 0.7 broadcast_in_dim.13.bias_ref
  1.4 0.7 broadcast_in_dim.15.db_ref
  2.1 0.7 broadcast_in_dim.14.ub_ref
  2.8 0.0 copy-start
  2.8 1.7 %copy-done = bf16[768,1536]{1,0:T(8,128)(2,1)S(1)} copy-done((bf16[768,1536]{1,0:T(8,128)(2,1)S(1)}, bf16[768,1536]{1,0:T(8,128)(2,1)}, u32[]{:S(2)}) %copy-start) | copy-done | bytes 2359320
  4.4 0.0 copy-start.1
  4.4 0.8 copy-done.1
  5.2 97.4 %shard_map.73 = bf16[3,8,768]{2,1,0:T(8,128)(2,1)S(1)} custom-call(bf16[3,8,768]{2,1,0:T(8,128)(2,1)S(1)} %bitcast.3, f32[1,768]{1,0:T(1,128)S(1)} %broadcast_in_dim.12.gain_ref, f32[1,768]{1,0:T(1,128)S(1)} %broadcast_in_dim.13.bias_ref, f32[1,1536]{1,0:T(1,128)S(1)} %broadcast_in_dim.14.ub_ref, f32[1,768]{1,0:T(1,128)S(1)} %broadcast_in_dim.15.db_ref, ...), custom_call_target="tpu_custom_call" | custom-call | tf_op jit(solution)/shard_map/pallas_call | solution.py:330
  102.7 0.6 copy.9
Async XLA Ops:
  2.8 1.7 %copy-start = (bf16[768,1536]{1,0:T(8,128)(2,1)S(1)}, bf16[768,1536]{1,0:T(8,128)(2,1)}, u32[]{:S(2)}) copy-start(bf16[768,1536]{1,0:T(8,128)(2,1)} %wu_hbm.1) | copy-start | bytes 7077892
  4.4 0.8 copy-start.1

commit v2 on v1

--- a/solution.py
+++ b/solution.py
@@ -12,18 +12,19 @@
 EPS = 1e-05
 J = 4
 SPLIT = ((0, 1), (2, 3))
-RS_ORDER = ((2, 3, 0, 1), (0, 1, 2, 3))
-AG_ORDER = ((0, 1, 2, 3), (2, 3, 0, 1))
+RS_ORDER = ((2, 0, 3, 1), (0, 2, 1, 3))
+LAST_ORDER = (0, 2, 1, 3)
+AG_ORDER = ((0, 2, 1, 3), (0, 2, 1, 3))
 GROUPS = 3
 
 
 def kernel(
     n,
-    x_ref, gain_ref, bias_ref, ub_ref, db_ref, wu_hbm, wd_hbm,
+    x_hbm, gain_hbm, bias_hbm, ub_hbm, db_hbm, wu_hbm, wd_hbm,
     out_ref,
-    wu, wd, xg, pbuf, lm, lm2, st_out, st_in, gb, gb_in, rs_out, rs_in, ag_own, ag_in,
+    x_ref, gain_ref, bias_ref, ub_ref, db_ref, wu, wd, xg, pbuf, lm, lm2, st_out, st_in, gb_rows, gb, gb_in, rs_out, rs_in, ag_own, ag_in,
     tb, pair_out, pair_in, star_out, star_in,
-    w_sem, x_ss, x_rs, st_ss, st_rs, gb_ss, gb_rs, r_ss, r_rs, a_ss, a_rs, p_ss, p_rs, s_ss, s_rs,
+    w_sem, x_ss, x_rs, f_ss, f_rs, st_ss, st_rs, gb_ss, gb_rs, r_ss, r_rs, a_ss, a_rs, p_ss, p_rs, s_ss, s_rs,
 ):
     half = n // 2
     feat, unit = wu.shape
@@ -45,22 +46,31 @@
     def drain(ref, sem):
         pltpu.make_async_copy(ref, ref, sem).wait()
 
-    load_up = pltpu.make_async_copy(wu_hbm, wu, w_sem.at[0])
-    load_down = pltpu.make_async_copy(wd_hbm, wd, w_sem.at[1])
-    load_up.start()
-    load_down.start()
+    load_x = pltpu.make_async_copy(x_hbm, x_ref, w_sem.at[0])
+    load_up = pltpu.make_async_copy(wu_hbm, wu, w_sem.at[1])
+    load_down = pltpu.make_async_copy(wd_hbm, wd, w_sem.at[2])
+    load_rows = [
+        pltpu.make_async_copy(src, dst.at[0], w_sem.at[3 + i])
+        for i, (src, dst) in enumerate(
+            ((gain_hbm, gain_ref), (bias_hbm, bias_ref), (ub_hbm, ub_ref), (db_hbm, db_ref))
+        )
+    ]
+    for load in (load_x, *load_rows, load_up, load_down):
+        load.start()
 
     barrier = pltpu.get_barrier_semaphore()
-    for to in along:
+    for to in (*along, sibling):
         pl.semaphore_signal(barrier, inc=1, device_id=to, device_id_type=MESH)
 
+    def peer(i):
+        return (z, 2 * lax.rem(q + i, n) + e)
+
     def greet(i, carry):
-        to = (z, lax.rem(c + i, 2 * n))
-        pl.semaphore_signal(barrier, inc=1, device_id=to, device_id_type=MESH)
+        pl.semaphore_signal(barrier, inc=1, device_id=peer(i), device_id_type=MESH)
         return carry
 
-    lax.fori_loop(1, 2 * n, greet, 0)
-    pl.semaphore_wait(barrier, 2 * n + 1)
+    lax.fori_loop(1, n, greet, 0)
+    pl.semaphore_wait(barrier, n + 2)
 
     def spread(far):
         for p in range(GROUPS):
@@ -73,11 +83,15 @@
                 pltpu.make_async_copy(x_ref.at[p], place, x_rs.at[k]).start()
 
                 def send(i, carry):
-                    to = (z, lax.rem(c + i, 2 * n))
-                    remote(x_ref.at[p], place, x_ss, x_rs.at[k], to).start()
+                    remote(x_ref.at[p], place, x_ss, x_rs.at[k], peer(i)).start()
                     return carry
 
-                lax.fori_loop(1, 2 * n, send, 0)
+                lax.fori_loop(1, n, send, 0)
+
+    def forward(k):
+        held = xg.at[pl.ds(k * 2 * GROUPS + e * GROUPS, GROUPS)]
+        drain(held, x_rs.at[k])
+        remote(held, held, f_ss, f_rs.at[k], sibling).start()
 
     def columns(tile):
         return jnp.concatenate([tile[:, g : g + 1][None] for g in range(2 * GROUPS)], axis=0)
@@ -101,7 +115,7 @@
         return lax.rem(z + n + half - s, n) if d == 0 else lax.rem(z + half + s, n)
 
     def wait_inputs(k):
-        drain(xg.at[pl.ds(k * 2 * GROUPS, 2 * GROUPS)], x_rs.at[k])
+        drain(xg.at[pl.ds(k * 2 * GROUPS, GROUPS)], f_rs.at[k])
 
     def products(s):
         wait_inputs(chunk(0, s))
@@ -132,16 +146,39 @@
         )
 
     per_row = unit // 128
+    gb_rows[...] = jnp.zeros_like(gb_rows)
     zero = jnp.zeros((rows, width), BF16)
     for d in range(2):
         for j in SPLIT[1 - d]:
             rs_in[d * half * J + j] = zero
 
-    spread(half)
-    spread(half - 1)
-    spread(half - 2)
-
+    load_x.wait()
+    def spread_all(i, carry):
+        spread(half - i)
+        return carry
+
+    lax.fori_loop(0, half + 1, spread_all, 0)
+
+    for load in load_rows:
+        load.wait()
     load_up.wait()
+    first = chunk(0, 0)
+    forward(first)
+    wait_inputs(first)
+    start = centered(first, 0)
+    st_out[0, 0] = lm[0] + pltpu.roll(lm2[0], 64, 1)
+    st_out[1, 0] = lm[0]
+    for d in range(2):
+        st_copy(d, 0).start()
+    for i in range(2):
+        for d in range(2):
+            j = SPLIT[d][i]
+            part = jnp.dot(start, wu[:, j * width : (j + 1) * width], preferred_element_type=F32)
+            rs_out[d * half * J + j] = part.astype(BF16)
+            rs_copy(d, 0, j).start()
+    for s in (1, 2):
+        for d in range(2):
+            forward(chunk(d, s))
     sub = lax.broadcasted_iota(jnp.int32, (16, feat), 0)
     gain, bias = gain_ref[...], bias_ref[...]
     gain_hi, bias_hi = gain.astype(BF16).astype(F32), bias.astype(BF16).astype(F32)
@@ -157,22 +194,9 @@
     sums = jnp.dot(lhs, wu[...], preferred_element_type=F32)
     for i in range(per_row):
         cols = slice(i * 128, (i + 1) * 128)
-        gb[i : i + 1] = sums[0:1, cols] + sums[1:2, cols]
-        gb[per_row + i : per_row + i + 1] = sums[2:3, cols] + sums[3:4, cols]
-
-    first = chunk(0, 0)
-    wait_inputs(first)
-    start = centered(first, 0)
-    st_out[0, 0] = lm[0] + pltpu.roll(lm2[0], 64, 1)
-    st_out[1, 0] = lm[0]
-    for d in range(2):
-        st_copy(d, 0).start()
-    for i in range(2):
-        for d in range(2):
-            j = SPLIT[d][i]
-            part = jnp.dot(start, wu[:, j * width : (j + 1) * width], preferred_element_type=F32)
-            rs_out[d * half * J + j] = part.astype(BF16)
-            rs_copy(d, 0, j).start()
+        gb_rows[i : i + 1] = sums[0:1, cols] + sums[1:2, cols]
+        gb_rows[per_row + i : per_row + i + 1] = sums[2:3, cols] + sums[3:4, cols]
+    gb[...] = gb_rows[...].astype(BF16)
     for d in range(2):
         gb_copy(d, 0, gb).start()
     products(1)
@@ -187,11 +211,11 @@
             st_out[d, s] = got + pltpu.roll(off, 32, 1) + pltpu.roll(square, 64, 1)
             st_copy(d, s).start()
             shift.append(columns(off))
-        own = gb[...]
+        own = gb_rows[...]
         for i in range(J):
             for d in range(2):
                 j = RS_ORDER[d][i]
-                if i < 2:
+                if j in SPLIT[1 - d]:
                     pl.when(s > 1)(lambda d=d, j=j: rs_copy(d, s - 1, j).wait_recv())
                 else:
                     rs_copy(d, s - 1, j).wait_recv()
@@ -208,7 +232,8 @@
         def _():
             gb_copy(1, s, gb_in.at[half + s - 1]).start()
 
-        spread(half - 2 - s)
+        pl.when(s < half - 1)(lambda: forward(chunk(0, s + 2)))
+        pl.when(s < half - 2)(lambda: forward(chunk(1, s + 2)))
         products(s + 1)
         return carry
 
@@ -220,10 +245,10 @@
 
     gb_copy(0, half - 1, gb).wait_recv()
     load_down.wait()
-    gb_all = gb[...]
+    own = gb_rows[...]
+    gb_all = own
     for i in range(2 * half - 1):
-        gb_all = gb_all + gb_in[i]
-    own = gb[...]
+        gb_all = gb_all + gb_in[i].astype(F32)
     for d in range(2):
         st_copy(d, half - 1).wait_recv()
     up, down = st_in[0, half - 1], st_in[1, half - 1]
@@ -232,7 +257,7 @@
     square = pltpu.roll(up + down, 64, 1) + lm2[0] + feat * off * off
     scale = lax.rsqrt(square * (1.0 / (n * feat)) - mean_off * mean_off + EPS)
     off_c, mean_c, scale_c = columns(off), columns(mean_off), columns(scale)
-    for j in range(J):
+    for j in LAST_ORDER:
         cols = slice(j * width, (j + 1) * width)
         total = pbuf[0:rows, cols].reshape(2 * GROUPS, 8, width)
         for d in range(2):
@@ -280,7 +305,7 @@
                 j = AG_ORDER[d][i]
                 ag_copy(d, s, j, ag_own.at[j]).wait_recv()
                 held = ag_in.at[(d * half + s) * J + j]
-                if i < 2:
+                if j in SPLIT[d]:
                     ag_copy(d, s + 1, j, held).start()
                 else:
                     pl.when(s < half - 2)(lambda d=d, j=j, held=held: ag_copy(d, s + 1, j, held).start())
@@ -313,7 +338,8 @@
         total = jnp.sum(star_in[p * n : (p + 1) * n].astype(F32), axis=0)
         out_ref[p] = (x_ref[p].astype(F32) + total + db_ref[...]).astype(BF16)
 
-    drain(xg.at[pl.ds(0, GROUPS * (2 * n - 1))], x_ss)
+    drain(xg.at[pl.ds(0, GROUPS * (n - 1))], x_ss)
+    drain(xg.at[pl.ds(0, GROUPS * n)], f_ss)
     drain(st_in, st_ss)
     drain(gb_in.at[pl.ds(0, n - 1)], gb_ss)
     drain(rs_in.at[pl.ds(0, (n - 1) * J)], r_ss)
@@ -325,14 +351,20 @@
 def local(n, inputs, ln_gain, ln_bias, w_up, up_bias, w_down, down_bias):
     feat, unit = w_up.shape
     half, rows, width = n // 2, 2 * GROUPS * 8, unit // J
-    vmem, hbm = pl.BlockSpec(memory_space=pltpu.VMEM), pl.BlockSpec(memory_space=pl.ANY)
+    tall = (2 * unit // 128 + 15) // 16 * 16
+    vmem, hbm = pl.BlockSpec(memory_space=pltpu.VMEM), pl.BlockSpec(memory_space=pltpu.HBM)
     sem = pltpu.SemaphoreType.DMA
     out = pl.pallas_call(
         functools.partial(kernel, n),
         out_shape=jax.ShapeDtypeStruct((GROUPS, 8, feat), BF16),
-        in_specs=[vmem] * 5 + [hbm] * 2,
+        in_specs=[hbm] * 7,
         out_specs=vmem,
         scratch_shapes=[
+            pltpu.VMEM((GROUPS, 8, feat), BF16),
+            pltpu.VMEM((1, feat), F32),
+            pltpu.VMEM((1, feat), F32),
+            pltpu.VMEM((1, unit), F32),
+            pltpu.VMEM((1, feat), F32),
             pltpu.VMEM((feat, unit), BF16),
             pltpu.VMEM((unit, feat), BF16),
             pltpu.VMEM((n * 2 * GROUPS, 8, feat), BF16),
@@ -341,8 +373,9 @@
             pltpu.VMEM((2, 8, 128), F32),
             pltpu.VMEM((2, half, 8, 128), F32),
             pltpu.VMEM((2, half, 8, 128), F32),
-            pltpu.VMEM((2 * unit // 128, 128), F32),
-            pltpu.VMEM((n, 2 * unit // 128, 128), F32),
+            pltpu.VMEM((tall, 128), F32),
+            pltpu.VMEM((tall, 128), BF16),
+            pltpu.VMEM((n, tall, 128), BF16),
             pltpu.VMEM((2 * half * J, rows, width), BF16),
             pltpu.VMEM((2 * half * J, rows, width), BF16),
             pltpu.VMEM((J, rows, width), BF16),
@@ -352,7 +385,9 @@
             pltpu.VMEM((n, GROUPS, 8, feat), BF16),
             pltpu.VMEM((n, GROUPS, 8, feat), BF16),
             pltpu.VMEM((GROUPS * n, 8, feat), BF16),
-            sem((2,)),
+            sem((7,)),
+            sem,
+            sem((n,)),
             sem,
             sem((n,)),
             sem,
@@ -372,13 +407,18 @@
             collective_id=0, has_side_effects=True, vmem_limit_bytes=50 << 20
         ),
     )(
-        inputs.reshape(GROUPS, 8, feat),
-        ln_gain[None],
-        ln_bias[None],
-        up_bias[None],
-        down_bias[None],
-        w_up,
-        w_down,
+        *(
+            pltpu.with_memory_space_constraint(a, pltpu.HBM)
+            for a in (
+                inputs.reshape(GROUPS, 8, feat),
+                ln_gain,
+                ln_bias,
+                up_bias,
+                down_bias,
+                w_up,
+                w_down,
+            )
+        )
     )
     return out.reshape(GROUPS * 8, feat)
 

time: 104 us -> 89.9 us (0.86)
  Pallas kernels: 97.4 us -> 89.2 us
  local copies, waits for them, and re-layouts: 5.82 us -> 0.62 us
    pallas_call x1, Pallas kernels: 97.4 us -> 89.2 us  [local(): pl.pallas_call(functools.partial(kernel, n), out_shape=jax.ShapeDtypeStru...]
    broadcast_in_dim x4 -> x0, local copies, waits for them, and re-layouts: 2.77 us -> none  [the longest x1 0.7 us: local(): up_bias[None]]
    unnamed x5 -> x1, local copies, waits for them, and re-layouts: 3.05 us -> 0.62 us
where the time goes in v2:
time: 89.9 us; the launch traced here: 89.8 us
  Pallas kernels  89.2 us (99%)
    pallas_call x1, Pallas kernels, local(): pl.pallas_call(functools.partial(kernel, n), out_shape=jax.ShapeDtypeStru...  89.2 us

profile of v2, /device:TPU:7, one launch (start us, length us, event | category | flops | bytes accessed | tf_op | source)
XLA Modules:
  0.0 89.8 jit_solution(18196570523135326545)
XLA Ops:
  0.0 89.2 %shard_map.73 = bf16[3,8,768]{2,1,0:T(8,128)(2,1)S(1)} custom-call(bf16[3,8,768]{2,1,0:T(8,128)(2,1)} %bitcast.3, f32[768]{0:T(1024)} %gain_hbm.1, f32[768]{0:T(1024)} %bias_hbm.1, f32[1536]{0:T(1024)} %ub_hbm.1, f32[768]{0:T(1024)} %db_hbm.1, bf16[768,1536]{1,0:T(8,128)(2,1)} %wu_hbm.1, bf16[1536,768]{1,0:T(8,128)(2,1)} %wd_hbm.1), custom_call_target="tpu_custom_call" | custom-call | tf_op jit(solution)/shard_map/pallas_call | solution.py:357
  89.2 0.6 copy.9

commit v3 on v2

--- a/solution.py
+++ b/solution.py
@@ -15,6 +15,7 @@
 RS_ORDER = ((2, 0, 3, 1), (0, 2, 1, 3))
 LAST_ORDER = (0, 2, 1, 3)
 AG_ORDER = ((0, 2, 1, 3), (0, 2, 1, 3))
+FAR_FIRST = (10, 9, 11, 6, 14, 8, 2, 5, 7, 13, 15, 1, 3, 4, 12)
 GROUPS = 3
 
 
@@ -63,7 +64,7 @@
         pl.semaphore_signal(barrier, inc=1, device_id=to, device_id_type=MESH)
 
     def peer(i):
-        return (z, 2 * lax.rem(q + i, n) + e)
+        return (z, 2 * lax.bitwise_xor(q, i) + e)
 
     def greet(i, carry):
         pl.semaphore_signal(barrier, inc=1, device_id=peer(i), device_id_type=MESH)
@@ -82,11 +83,8 @@
                 place = xg.at[k * 2 * GROUPS + e * GROUPS + p]
                 pltpu.make_async_copy(x_ref.at[p], place, x_rs.at[k]).start()
 
-                def send(i, carry):
+                for i in FAR_FIRST:
                     remote(x_ref.at[p], place, x_ss, x_rs.at[k], peer(i)).start()
-                    return carry
-
-                lax.fori_loop(1, n, send, 0)
 
     def forward(k):
         held = xg.at[pl.ds(k * 2 * GROUPS + e * GROUPS, GROUPS)]
@@ -199,19 +197,31 @@
     gb[...] = gb_rows[...].astype(BF16)
     for d in range(2):
         gb_copy(d, 0, gb).start()
-    products(1)
-
-    def rs_step(s, carry):
-        shift = []
+    own_row = jnp.concatenate([gb_rows[i : i + 1] for i in range(per_row)], axis=1)
+
+    def shifted(s):
         for d in range(2):
             st_copy(d, s - 1).wait_recv()
             got = st_in[d, s - 1]
             off = jnp.where(head, lm[d] - got, 0.0)
-            square = jnp.where(head, lm2[d] + feat * off * off, 0.0)
-            st_out[d, s] = got + pltpu.roll(off, 32, 1) + pltpu.roll(square, 64, 1)
-            st_copy(d, s).start()
-            shift.append(columns(off))
-        own = gb_rows[...]
+
+            @pl.when(s < half)
+            def _():
+                square = jnp.where(head, lm2[d] + feat * off * off, 0.0)
+                st_out[d, s] = got + pltpu.roll(off, 32, 1) + pltpu.roll(square, 64, 1)
+                st_copy(d, s).start()
+
+            off_c = columns(off)
+            for j in range(J):
+                cols = slice(j * width, (j + 1) * width)
+                at = slice(d * rows, (d + 1) * rows)
+                mine = pbuf[at, cols].reshape(2 * GROUPS, 8, width) + off_c * own_row[:, cols][None]
+                pbuf[at, cols] = mine.reshape(rows, width)
+
+    products(1)
+    shifted(1)
+
+    def rs_step(s, carry):
         for i in range(J):
             for d in range(2):
                 j = RS_ORDER[d][i]
@@ -221,7 +231,7 @@
                     rs_copy(d, s - 1, j).wait_recv()
                 got = rs_in[(d * half + s - 1) * J + j].astype(F32).reshape(2 * GROUPS, 8, width)
                 mine = pbuf[d * rows : (d + 1) * rows, j * width : (j + 1) * width]
-                total = got + mine.reshape(2 * GROUPS, 8, width) + shift[d] * row_of(own, 0, j)[None]
+                total = got + mine.reshape(2 * GROUPS, 8, width)
                 rs_out[(d * half + s) * J + j] = total.reshape(rows, width).astype(BF16)
                 rs_copy(d, s, j).start()
         gb_copy(0, s - 1, gb).wait_recv()
@@ -235,6 +245,7 @@
         pl.when(s < half - 1)(lambda: forward(chunk(0, s + 2)))
         pl.when(s < half - 2)(lambda: forward(chunk(1, s + 2)))
         products(s + 1)
+        shifted(s + 1)
         return carry
 
     lax.fori_loop(1, half, rs_step, 0)
@@ -245,18 +256,15 @@
 
     gb_copy(0, half - 1, gb).wait_recv()
     load_down.wait()
-    own = gb_rows[...]
-    gb_all = own
+    gb_all = gb_rows[...]
     for i in range(2 * half - 1):
         gb_all = gb_all + gb_in[i].astype(F32)
-    for d in range(2):
-        st_copy(d, half - 1).wait_recv()
     up, down = st_in[0, half - 1], st_in[1, half - 1]
     off = jnp.where(head, lm[0] - up, 0.0)
     mean_off = (pltpu.roll(up + down, 96, 1) + off) * (1.0 / n)
     square = pltpu.roll(up + down, 64, 1) + lm2[0] + feat * off * off
     scale = lax.rsqrt(square * (1.0 / (n * feat)) - mean_off * mean_off + EPS)
-    off_c, mean_c, scale_c = columns(off), columns(mean_off), columns(scale)
+    mean_c, scale_c = columns(mean_off), columns(scale)
     for j in LAST_ORDER:
         cols = slice(j * width, (j + 1) * width)
         total = pbuf[0:rows, cols].reshape(2 * GROUPS, 8, width)
@@ -264,7 +272,7 @@
             rs_copy(d, half - 1, j).wait_recv()
             got = rs_in[(d * half + half - 1) * J + j]
             total = total + got.astype(F32).reshape(2 * GROUPS, 8, width)
-        total = total + off_c * row_of(own, 0, j)[None] - mean_c * row_of(gb_all, 0, j)[None]
+        total = total - mean_c * row_of(gb_all, 0, j)[None]
         v = total * scale_c + row_of(gb_all, per_row, j)[None] + ub_ref[:, cols][None]
         hidden = jax.nn.gelu(v, approximate=True)
         ag_own[j] = hidden.reshape(rows, width).astype(BF16)

time: 89.9 us -> 89.2 us (level)
  no operation moved by 1% of the time
where the time goes in v3:
time: 89.2 us; the launch traced here: 89.1 us
  Pallas kernels  88.5 us (99%)
    pallas_call x1, Pallas kernels, local(): pl.pallas_call(functools.partial(kernel, n), out_shape=jax.ShapeDtypeStru...  88.5 us

profile of v3, /device:TPU:7, one launch (start us, length us, event | category | flops | bytes accessed | tf_op | source)
XLA Modules:
  0.0 89.1 jit_solution(11899508106603066938)
XLA Ops:
  0.0 88.5 %shard_map.73 = bf16[3,8,768]{2,1,0:T(8,128)(2,1)S(1)} custom-call(bf16[3,8,768]{2,1,0:T(8,128)(2,1)} %bitcast.3, f32[768]{0:T(1024)} %gain_hbm.1, f32[768]{0:T(1024)} %bias_hbm.1, f32[1536]{0:T(1024)} %ub_hbm.1, f32[768]{0:T(1024)} %db_hbm.1, bf16[768,1536]{1,0:T(8,128)(2,1)} %wu_hbm.1, bf16[1536,768]{1,0:T(8,128)(2,1)} %wd_hbm.1), custom_call_target="tpu_custom_call" | custom-call | tf_op jit(solution)/shard_map/pallas_call | solution.py:365
  88.5 0.6 copy.9

commit v4 on v3

--- a/solution.py
+++ b/solution.py
@@ -332,13 +332,18 @@
     lax.fori_loop(0, half - 1, ag_step, 0)
     to_owner(lax.rem(z + 1 + half, n))
     to_owner(lax.rem(z + half - 1, n))
-    pieces = []
-    for d in range(2):
-        for j in SPLIT[d]:
+    last = lax.rem(z + half, n)
+    value = jnp.zeros((rows, feat), F32)
+    for i in range(2):
+        for d in range(2):
+            j = SPLIT[d][i]
             ag_copy(d, half - 1, j, ag_own.at[j]).wait_recv()
-            pieces.append(ag_in[(d * half + half - 1) * J + j])
-    last = lax.rem(z + half, n)
-    to_pair(last, down_product(pieces))
+            value = value + jnp.dot(
+                ag_in[(d * half + half - 1) * J + j],
+                wd[j * width : (j + 1) * width],
+                preferred_element_type=F32,
+            )
+    to_pair(last, value)
     to_owner(last)
 
     drain(star_in, s_rs)

time: 89.2 us -> 89.2 us (level)
  no operation moved by 1% of the time
where the time goes in v4:
time: 89.2 us; the launch traced here: 89.1 us
  Pallas kernels  88.4 us (99%)
    pallas_call x1, Pallas kernels, local(): pl.pallas_call(functools.partial(kernel, n), out_shape=jax.ShapeDtypeStru...  88.4 us

profile of v4, /device:TPU:7, one launch (start us, length us, event | category | flops | bytes accessed | tf_op | source)
XLA Modules:
  0.0 89.1 jit_solution(14690374229536877405)
XLA Ops:
  0.0 88.4 %shard_map.73 = bf16[3,8,768]{2,1,0:T(8,128)(2,1)S(1)} custom-call(bf16[3,8,768]{2,1,0:T(8,128)(2,1)} %bitcast.3, f32[768]{0:T(1024)} %gain_hbm.1, f32[768]{0:T(1024)} %bias_hbm.1, f32[1536]{0:T(1024)} %ub_hbm.1, f32[768]{0:T(1024)} %db_hbm.1, bf16[768,1536]{1,0:T(8,128)(2,1)} %wu_hbm.1, bf16[1536,768]{1,0:T(8,128)(2,1)} %wd_hbm.1), custom_call_target="tpu_custom_call" | custom-call | tf_op jit(solution)/shard_map/pallas_call | solution.py:370
  88.4 0.6 copy.9
